TPU v7x, 128 devices: a whole 4x4x4 slice. The times are simulated.
128 devices in a mesh: expert: 32 (over z, y, core), tensor: 4 (over x).
Axes of the slice: x: 4, y: 4, z: 4, core: 2. Of those that a mesh axis runs over, the one named last changes fastest.
Arguments:
- activations: bfloat16 [4096, 7168], P('expert', 'tensor'), may hold values from -6 to 6
- cotangent: bfloat16 [4096, 7168], P('expert', 'tensor'), may hold values from -6 to 6
- expert_ids: int32 [4096, 8], P('expert'), may hold values from 0 to 31, all different within a row; in each aligned block of 128 rows (0 to 127, 128 to 255, ...) at most 40 rows name the same one
- combine: float32 [4096, 8], P('expert'), may hold values from 0.1 to 0.6
- log_ratio: float32 [4096], P('expert'), may hold values from -3 to 3
- valid_mask: int32 [4096], P('expert'), may hold values from 0 to 1, as said below
- segment_ids: int32 [4096], P('expert'), may hold values from 0 to 63, as said below
- w_gate: bfloat16 [32, 7168, 1024], P('expert', 'tensor'), may hold values from -0.0625 to 0.0625
- w_up: bfloat16 [32, 7168, 1024], P('expert', 'tensor'), may hold values from -0.0625 to 0.0625
- w_down: bfloat16 [32, 1024, 7168], P('expert', None, 'tensor'), may hold values from -0.1875 to 0.1875
Outputs:
- input_grad: bfloat16 [4096, 7168], P('expert', 'tensor')
- down_grad: bfloat16 [32, 1024, 7168], P('expert', None, 'tensor')
Inputs may be any that keep to these rules, and one draw needn't show every extreme that they name: `expert_ids`: among the 128 tokens of one index of expert, each expert is named at most 40 times. `valid_mask`: 0 at the last of the 128 tokens of every index of expert. `segment_ids`: never falling; no sequence begins at the first token of an index of expert other than index 0; each sequence has 1 to 254 tokens.
All inputs are finite; a program needn't handle non-finite values.
Results may differ from a plain program's by a relative error of at most 0.0064.
Values may be sent and summed in bfloat16 or wider, within the bound.
A program may use at most 128 MiB of HBM per device.

v0:
```python
import jax
import jax.numpy as jnp
from jax import lax
from jax.sharding import PartitionSpec as P


def shifted(x, axis, by):
    peers = lax.axis_size(axis)
    pairs = [(i, i + by) for i in range(peers) if 0 <= i + by < peers]
    return lax.ppermute(x, axis, pairs)


def pointwise(gate_pre, up_pre, down_pre, scale_rows):
    sigmoid_val = jax.nn.sigmoid(gate_pre)
    activated = gate_pre * sigmoid_val
    slope = sigmoid_val * (1.0 + gate_pre * (1.0 - sigmoid_val))
    scaled_dh = down_pre * scale_rows
    hidden_scaled = (activated * up_pre * scale_rows).astype(jnp.bfloat16)
    grad_gate = (scaled_dh * up_pre * slope).astype(jnp.bfloat16)
    grad_up = (scaled_dh * activated).astype(jnp.bfloat16)
    return (hidden_scaled, grad_gate, grad_up)


def local(
    activations,
    cotangent,
    expert_ids,
    combine,
    log_ratio,
    valid_mask,
    segment_ids,
    w_gate,
    w_up,
    w_down,
):
    groups = lax.axis_size("expert")
    tok_rows, quarter = activations.shape
    top_count = expert_ids.shape[1]
    capacity = min(tok_rows, tok_rows * top_count // groups * 5 // 4)
    slot_total = tok_rows * top_count
    starts = shifted(segment_ids[:1] + 1, "expert", -1)
    following = jnp.concatenate([segment_ids[1:], starts - 1])
    live_mask = jnp.maximum(valid_mask, (following != segment_ids).astype(jnp.int32))
    live_total = lax.psum(jnp.sum(live_mask.astype(jnp.float32)), "expert")
    factor = tok_rows * groups / live_total
    weight = jnp.minimum(jnp.exp(log_ratio), 2.0) * live_mask.astype(jnp.float32)
    slot_scale = (combine * weight[:, None]).astype(jnp.bfloat16)
    flat_ids = expert_ids.reshape(-1)
    onehot = (flat_ids[:, None] == jnp.arange(groups, dtype=jnp.int32)[None, :]).astype(jnp.int32)
    position = jnp.sum((jnp.cumsum(onehot, axis=0) - onehot) * onehot, axis=1)
    target = flat_ids * capacity + position
    source = (
        jnp.zeros((groups * capacity,), jnp.int32)
        .at[target]
        .set(jnp.arange(1, slot_total + 1, dtype=jnp.int32))
    )
    filled = source > 0
    slot_index = jnp.maximum(source - 1, 0)
    token_index = slot_index // top_count
    send_act = jnp.where(filled[:, None], activations[token_index], 0).reshape(
        groups, capacity, quarter
    )
    send_cot = jnp.where(filled[:, None], cotangent[token_index], 0).reshape(
        groups, capacity, quarter
    )
    send_scale = jnp.where(filled, slot_scale.reshape(-1)[slot_index], 0).reshape(groups, capacity)
    recv_act, recv_cot, recv_scale = (
        lax.all_to_all(send_act, "expert", split_axis=0, concat_axis=0, tiled=True),
        lax.all_to_all(send_cot, "expert", split_axis=0, concat_axis=0, tiled=True),
        lax.all_to_all(send_scale, "expert", split_axis=0, concat_axis=0, tiled=True),
    )
    rows_act = recv_act.reshape(-1, quarter)
    rows_cot = recv_cot.reshape(-1, quarter)
    rows_scale = recv_scale.reshape(-1).astype(jnp.float32)[None, :]
    row_total = rows_act.shape[0]
    gate_mat = w_gate[0]
    up_mat = w_up[0]
    down_mat = w_down[0]
    contract_first = (((0,), (1,)), ((), ()))
    contract_last = (((1,), (1,)), ((), ()))
    gate_part = lax.dot_general(
        gate_mat, rows_act, contract_first, preferred_element_type=jnp.float32
    )
    up_part = lax.dot_general(up_mat, rows_act, contract_first, preferred_element_type=jnp.float32)
    down_part = lax.dot_general(
        down_mat, rows_cot, contract_last, preferred_element_type=jnp.float32
    )
    summed, down_pre = lax.psum(
        (jnp.concatenate([gate_part, up_part], axis=1), down_part), "tensor"
    )
    hidden_scaled, grad_gate, grad_up = pointwise(
        summed[:, :row_total], summed[:, row_total:], down_pre, rows_scale
    )
    down_sum = jnp.dot(hidden_scaled, rows_cot, preferred_element_type=jnp.float32)
    row_grads = lax.dot_general(
        grad_gate, gate_mat, contract_first, preferred_element_type=jnp.float32
    )
    row_grads = row_grads + lax.dot_general(
        grad_up, up_mat, contract_first, preferred_element_type=jnp.float32
    )
    outgoing = row_grads.astype(jnp.bfloat16).reshape(groups, capacity, quarter)
    returned = lax.all_to_all(outgoing, "expert", split_axis=0, concat_axis=0, tiled=True).reshape(
        -1, quarter
    )
    per_slot = returned[target].reshape(tok_rows, top_count, quarter).astype(jnp.float32)
    input_grad = (jnp.sum(per_slot, axis=1) * factor).astype(jnp.bfloat16)
    down_grad = (down_sum * factor).astype(jnp.bfloat16)[None]
    return (input_grad, down_grad)


def solution(mesh):
    return jax.shard_map(
        local,
        mesh=mesh,
        in_specs=(
            P("expert", "tensor"),
            P("expert", "tensor"),
            P("expert", None),
            P("expert", None),
            P("expert"),
            P("expert"),
            P("expert"),
            P("expert", "tensor", None),
            P("expert", "tensor", None),
            P("expert", None, "tensor"),
        ),
        out_specs=(P("expert", "tensor"), P("expert", None, "tensor")),
        check_vma=False,
    )
```

profile of v0, /device:TPU:0, one launch (start us, length us, event | category | flops | bytes accessed | tf_op | source)
XLA Modules:
  0.0 653.5 jit_solution(11766333205553723969)
XLA Ops:
  7.9 1.3 collective-permute-start
  11.6 9.0 %reduce-window.6 = s32[32,8,128]{2,1,0:T(8,128)S(1)} reduce-window(s32[32,8,128]{2,1,0:T(8,128)S(1)} %fusion.16, s32[]{:T(128)} %constant.18.clone.1), window={size=1x1x128 pad=0_0x0_0x127_0}, to_apply=%region_0.0 | reduce-window | flops 4161536 | bytes 262148 | tf_op jit(solution)/shard_map/reduce-window
  21.3 4.3 scatter_custom_fusion
  25.7 5.8 gather_fusion
  31.5 5.9 gather_fusion.2
  39.0 8.0 %gather_fusion.1 = bf16[1280]{0:T(1024)(128)(2,1)S(1)} fusion(bf16[1024]{0:T(1024)(128)(2,1)S(1)} %reshape.98, s32[2048]{0:T(1024)S(1)} %get-tuple-element.12), kind=kCustom, calls=%fused_computation.1 | custom fusion | bytes 10240 | tf_op jit(solution)/shard_map/gather | solution.py:66
  47.0 5.5 broadcast_select_fusion.1
  52.6 65.5 %all_to_all.25 = bf16[32,40,1792]{2,1,0:T(8,128)(2,1)} all-to-all(bf16[32,40,1792]{2,1,0:T(8,128)(2,1)S(1)} %get-tuple-element.11), channel_id=1, replica_groups=mesh['expert'=32,'tensor'=4] {'expert'}, dimensions={0} | all-to-all | bytes 9175040 | tf_op jit(solution)/shard_map/all_to_all | solution.py:68
  118.0 5.0 all-to-all-start
  123.6 10.8 %convolution_bitcast_fusion = f32[1024,1280]{0,1:T(8,128)} fusion(bf16[1280,1792]{1,0:T(8,128)(2,1)} %bitcast.58, bf16[1,1792,1024]{2,1,0:T(8,128)(2,1)} %param.18), kind=kOutput, calls=%fused_computation.16 | convolution fusion | flops 4697620480 | bytes 13500416 | tf_op jit(solution)/shard_map/dot_general | solution.py:84
  134.4 6.7 %convolution_bitcast_fusion.1 = f32[1024,1280]{0,1:T(8,128)} fusion(bf16[1280,1792]{1,0:T(8,128)(2,1)S(1)} %bitcast.61, bf16[1,1792,1024]{2,1,0:T(8,128)(2,1)S(1)} %copy-done.7), kind=kOutput, calls=%fused_computation.17 | convolution fusion | flops 4697620480 | bytes 13500416 | tf_op jit(solution)/shard_map/dot_general | solution.py:81
  141.1 10.1 %pad_maximum_fusion = f32[1024,2560]{0,1:T(8,128)} fusion(f32[1024,1280]{0,1:T(8,128)} %convolution_bitcast_fusion, f32[1024,1280]{0,1:T(8,128)} %convolution_bitcast_fusion.1), kind=kLoop, calls=%fused_computation.5 | loop fusion | flops 2621440 | bytes 20971520 | tf_op jit(solution)/shard_map/concatenate | solution.py:89
  151.2 30.1 %all-to-all-done = bf16[32,40,1792]{2,1,0:T(8,128)(2,1)} async-done(((bf16[32,40,1792]{2,1,0:T(8,128)(2,1)}), bf16[32,40,1792]{2,1,0:T(8,128)(2,1)}, u32[]{:S(2)}, u32[]{:S(2)}) %all-to-all-start) | async-done | bytes 4587552 | tf_op jit(solution)/shard_map/all_to_all | solution.py:69
  181.3 10.8 %convolution_bitcast_fusion.2 = f32[1024,1280]{0,1:T(8,128)} fusion(bf16[1280,1792]{1,0:T(8,128)(2,1)} %bitcast.5, bf16[1,1024,1792]{2,1,0:T(8,128)(2,1)} %param.19), kind=kOutput, calls=%fused_computation.18 | convolution fusion | flops 4697620480 | bytes 13500416 | tf_op jit(solution)/shard_map/dot_general | solution.py:85
  192.2 10.5 %all_to_all.26 = bf16[32,1,40]{2,1,0:T(2,128)(2,1)S(1)} all-to-all(bf16[32,1,40]{2,1,0:T(2,128)(2,1)S(1)} %all_to_all.20), channel_id=1, replica_groups=mesh['expert'=32,'tensor'=4] {'expert'}, dimensions={0} | all-to-all | bytes 5120 | tf_op jit(solution)/shard_map/all_to_all | solution.py:70
  202.9 264.9 %all-reduce.3.cloned.1.call-done = (f32[1024,2560]{0,1:T(8,128)}, f32[1024,1280]{0,1:T(8,128)}) async-done(((f32[1024,2560]{0,1:T(8,128)}, f32[1024,1280]{0,1:T(8,128)}), (f32[1024,2560]{0,1:T(8,128)}, f32[1024,1280]{0,1:T(8,128)})) %all-reduce.3.cloned.1.call-update) | async-done | bytes 15728656 | tf_op jit(solution)/shard_map/psum | solution.py:88
  467.8 16.8 %fusion.3 = f32[1280,1792]{1,0:T(8,128)} fusion(bf16[1,1792,1024]{2,1,0:T(8,128)(2,1)} %param.17, f32[1024,2560]{0,1:T(8,128)} %get-tuple-element.2, f32[1024,1280]{0,1:T(8,128)} %get-tuple-element.3, f32[1280]{0:T(1024)S(1)} %reshape.102), kind=kOutput, calls=%fused_computation.21 | convolution fusion | flops 4712038400 | bytes 28578816 | tf_op jit(solution)/shard_map/dot_general | solution.py:95
  484.6 14.3 %add_convert_fusion = bf16[1280,1792]{1,0:T(8,128)(2,1)} fusion(f32[1280,1792]{1,0:T(8,128)} %fusion.3, bf16[1,1792,1024]{2,1,0:T(8,128)(2,1)} %param.18, f32[1024,1280]{0,1:T(8,128)S(1)} %copy-done.6, f32[1280]{0:T(1024)S(1)} %reshape.102, f32[1024,2560]{0,1:T(8,128)} %get-tuple-element.2), kind=kOutput, calls=%fused_computation.6 | convolution fusion | flops 4711383040 | bytes 27923456 | tf_op jit(solution)/shard_map/dot_general | solution.py:98
  498.9 7.4 %all-to-all-start.3 = ((bf16[32,40,1792]{2,1,0:T(8,128)(2,1)}), bf16[32,40,1792]{2,1,0:T(8,128)(2,1)}, u32[]{:S(2)}, u32[]{:S(2)}) async-start(bf16[32,40,1792]{2,1,0:T(8,128)(2,1)} %bitcast.57), calls=%async_computation.3 | async-start | bytes 9175040 | tf_op jit(solution)/shard_map/all_to_all | solution.py:102
  506.3 110.4 %psum.23 = f32[]{:T(128)} all-reduce(f32[]{:T(128)} %get-tuple-element.4), channel_id=1, replica_groups=mesh['expert'=32,'tensor'=4] {'expert'}, use_global_device_ids=true, to_apply=%region_8.9 | all-reduce | flops 1 | bytes 8 | tf_op jit(solution)/shard_map/psum | solution.py:44
  617.4 12.9 %fusion.7 = bf16[1,1024,1792]{2,1,0:T(8,128)(2,1)} fusion(f32[]{:T(128)S(6)} %div.17, bf16[1280,1792]{1,0:T(8,128)(2,1)} %bitcast.5, f32[1024,2560]{0,1:T(8,128)} %get-tuple-element.2, f32[1280]{0:T(1024)S(1)} %reshape.102), kind=kOutput, calls=%fused_computation.25 | convolution fusion | flops 4710465536 | bytes 18748420 | tf_op jit(solution)/shard_map/dot_general | solution.py:94
  630.2 10.9 %gather_fusion.3 = bf16[1024,1792]{1,0:T(8,128)(2,1)} fusion(bf16[1280,1792]{1,0:T(8,128)(2,1)} %bitcast.15, s32[1024]{0:T(1024)S(1)} %broadcast_clamp_fusion), kind=kCustom, calls=%fused_computation.3 | custom fusion | bytes 7344128 | tf_op jit(solution)/shard_map/gather | solution.py:105
  641.1 4.5 convert_reduce_fusion
  645.6 0.8 multiply_convert_fusion.7
  (57 shorter events, 4.9 us)
Async XLA Ops:
  7.2 18.5 %copy-start = (bf16[128,1792]{1,0:T(8,128)(2,1)S(1)}, bf16[128,1792]{1,0:T(8,128)(2,1)}, u32[]{:S(2)}) copy-start(bf16[128,1792]{1,0:T(8,128)(2,1)} %param.11) | copy-start | bytes 1376260
  7.9 29.5 %collective-permute-start = (s32[1]{0:T(128)}, s32[1]{0:T(128)}, u32[]{:S(2)}, u32[]{:S(2)}) collective-permute-start(s32[1]{0:T(128)} %add.59), channel_id=1, source_target_pairs={{4,0},{8,4},{12,8},{16,12},{20,16},{24,20},{28,24},{32,28},{36,32}... | collective-permute-start | bytes 20 | tf_op jit(solution)/shard_map/ppermute | solution.py:10
  25.7 5.8 copy-start.2
  31.5 6.5 copy-start.4
  31.5 6.5 copy-start.5
  31.5 7.2 %copy-start.8 = (f32[128]{0:T(128)S(1)}, f32[128]{0:T(128)}, u32[]{:S(2)}) copy-start(f32[128]{0:T(128)} %param.14) | copy-start | bytes 1540
  31.5 7.2 %copy-start.3 = (f32[128,8]{0,1:T(8,128)S(1)}, f32[128,8]{0,1:T(8,128)}, u32[]{:S(2)}) copy-start(f32[128,8]{0,1:T(8,128)} %param.13) | copy-start | bytes 12292
  118.0 16.3 %slice-start = ((s8[4587520]{0:T(1024)(128)(4,1)}), s8[393216]{0:T(1024)(128)(4,1)S(1)}, s32[]{:S(2)}) async-start(s8[4587520]{0:T(1024)(128)(4,1)} %bitcast.59), calls=%async_computation.5 | async-start | bytes 786432
  118.0 63.2 %all-to-all-start = ((bf16[32,40,1792]{2,1,0:T(8,128)(2,1)}), bf16[32,40,1792]{2,1,0:T(8,128)(2,1)}, u32[]{:S(2)}, u32[]{:S(2)}) async-start(bf16[32,40,1792]{2,1,0:T(8,128)(2,1)} %get-tuple-element.10), calls=%async_computation | async-start | bytes 9175040 | tf_op jit(solution)/shard_map/all_to_all | solution.py:69
  123.0 344.7 %all-reduce.3.cloned.1.call-start = ((), (), s32[]{:S(2)}) async-start(), calls=%async_computation.4 | async-start | bytes 31457280 | tf_op jit(solution)/shard_map/psum | solution.py:88
  123.6 10.8 %slice-start.1 = ((s8[4587520]{0:T(1024)(128)(4,1)}), s8[4194304]{0:T(1024)(128)(4,1)S(1)}, s32[]{:S(2)}) async-start(s8[4587520]{0:T(1024)(128)(4,1)} %bitcast.59), calls=%async_computation.6 | async-start | bytes 8388608
  123.6 10.8 %copy-start.7 = (bf16[1,1792,1024]{2,1,0:T(8,128)(2,1)S(1)}, bf16[1,1792,1024]{2,1,0:T(8,128)(2,1)}, u32[]{:S(2)}) copy-start(bf16[1,1792,1024]{2,1,0:T(8,128)(2,1)} %param.17) | copy-start | bytes 11010052
  467.8 16.8 %copy-start.6 = (f32[1024,1280]{0,1:T(8,128)S(1)}, f32[1024,1280]{0,1:T(8,128)}, u32[]{:S(2)}) copy-start(f32[1024,1280]{0,1:T(8,128)} %get-tuple-element.3) | copy-start | bytes 15728644
  498.9 131.4 %all-to-all-start.3 = ((bf16[32,40,1792]{2,1,0:T(8,128)(2,1)}), bf16[32,40,1792]{2,1,0:T(8,128)(2,1)}, u32[]{:S(2)}, u32[]{:S(2)}) async-start(bf16[32,40,1792]{2,1,0:T(8,128)(2,1)} %bitcast.57), calls=%async_computation.3 | async-start | bytes 9175040 | tf_op jit(solution)/shard_map/all_to_all | solution.py:102
  630.2 16.2 %copy-start.1 = (bf16[128,1792]{1,0:T(8,128)(2,1)S(1)}, bf16[128,1792]{1,0:T(8,128)(2,1)}, u32[]{:S(2)}) copy-start(bf16[128,1792]{1,0:T(8,128)(2,1)} %param.11) | copy-start | bytes 1376260
Sparse Core Ops, SparseCore 0:
  192.2 275.5 all-reduce.2
where the time goes:
time: 658 us; the launch traced here: 654 us
  waiting for transfers between devices  295 us (45%)
  blocking collectives  186 us (28%)
  matrix products  72.2 us (11%)
  local copies, waits for them, and re-layouts  37.6 us (6%)
  other arithmetic  31.6 us (5%)
  between operations  16.5 us (3%)
  starting transfers between devices  14.2 us (2%)
    psum x1, waiting for transfers between devices, local(): lax.psum((jnp.concatenate([gate_part, up_part], axis=1), down_part), 'ten...  265 us
    psum x1, blocking collectives, local(): live_total = lax.psum(jnp.sum(live_mask.astype(jnp.float32)), 'expert')  110 us
    all_to_all x1, blocking collectives, local(): lax.all_to_all(send_act, 'expert', split_axis=0, concat_axis=0, tiled=True)  65.5 us
    all_to_all x1, waiting for transfers between devices, local(): lax.all_to_all(send_cot, 'expert', split_axis=0, concat_axis=0, tiled=True)  30.1 us
    dot_general x1, matrix products, local(): lax.dot_general(grad_gate, gate_mat, contract_first, preferred_element_ty...  16.8 us
    dot_general x1, matrix products, local(): lax.dot_general(grad_up, up_mat, contract_first, preferred_element_type=j...  14.3 us
  transfers between devices with their start and end apart: 4, of which 2 were waited for; matrix products, arithmetic and copies ran while one was open for 11% of the time, Pallas kernels for 0%

commit v1 on v0

v1 whole, which is shorter than its diff:
```python
import functools

import jax
import jax.numpy as jnp
from jax import lax
from jax.experimental import pallas as pl
from jax.experimental.pallas import tpu as pltpu
from jax.sharding import PartitionSpec as P

BF = jnp.bfloat16
F32 = jnp.float32
MESH = pl.DeviceIdType.MESH

SIDE = 4
CHIPS = SIDE * SIDE
CAP = 40
TOK = 128
ROWS = 2 * CAP
TOP = 8
GROUP = 2
CHUNKS = CHIPS // GROUP
R = GROUP * ROWS
HID = 128
BLOCK = 2 * TOK + 16

ORDER = [
    (0, 0), (3, 0), (1, 0), (0, 3), (0, 1), (3, 3), (1, 1), (3, 1),
    (1, 3), (2, 0), (0, 2), (3, 2), (2, 3), (1, 2), (2, 1), (2, 2),
]
EVENTS = [
    [(3, 0), (0, 3), (1, 0), (0, 1)],
    [],
    [(3, 3), (2, 0)],
    [(1, 3), (3, 1), (1, 1)],
    [(0, 2)],
    [(2, 3), (2, 1), (3, 2)],
    [(1, 2)],
    [(2, 2)],
]
HALVES = (pl.ds(0, TOK), pl.ds(TOK, BLOCK - TOK))


def dot(a, b, ca, cb):
    return lax.dot_general(a, b, (((ca,), (cb,)), ((), ())), preferred_element_type=F32)


def kernel(
    blk, w_gate, w_up, w_down,
    in_grad, down_grad, gbuf,
    wgu, wd, stage, rowact, rowcot, scl, part, own, r1, r2, ag, hs, rets, retr, dense, sibr, sall,
    dgt, igt, cnt,
    wsem, stsem, gsend, grecv, bsend, brecv, r1s, r1r, r2s, r2r, a1s, a1r, a2s, a2r, rts, rtr,
    css, csr, osem,
):
    e = lax.axis_index("expert")
    x = lax.axis_index("tensor")
    c = lax.rem(e, 2)
    chip = lax.div(e, 2)
    z = lax.div(chip, SIDE)
    y = lax.rem(chip, SIDE)
    width = blk.shape[1]
    right = lax.rem(x + 1, SIDE)
    left = lax.rem(x + SIDE - 1, SIDE)

    def chip_at(dz, dy):
        return lax.rem(z + dz, SIDE) * SIDE + lax.rem(y + dy, SIDE)

    def peer(dz, dy):
        return (chip_at(dz, dy) * 2 + c, x)

    sibling = (chip * 2 + 1 - c, x)

    def zy(da, db):
        return da * (1 - c) + db * c, da * c + db * (1 - c)

    def slot(da, db):
        dz, dy = zy(da % SIDE, db % SIDE)
        return dz * SIDE + dy

    bar = pltpu.get_barrier_semaphore()
    partners = [(e, right), (e, left), sibling]
    partners += [peer(dz, dy) for dz in range(SIDE) for dy in range(SIDE) if (dz, dy) != (0, 0)]
    for p in partners:
        pl.semaphore_signal(bar, inc=1, device_id=p, device_id_type=MESH)

    wcopies = []
    for g in range(8):
        cols = pl.ds(g * HID, HID)
        wcopies.append(
            pltpu.make_async_copy(w_gate.at[0, :, cols], wgu.at[:, pl.ds(2 * g * HID, HID)], wsem.at[2 * g])
        )
        wcopies.append(
            pltpu.make_async_copy(w_up.at[0, :, cols], wgu.at[:, pl.ds((2 * g + 1) * HID, HID)], wsem.at[2 * g + 1])
        )
    wcopies.append(pltpu.make_async_copy(w_down.at[0], wd, wsem.at[16]))
    for cp in wcopies:
        cp.start()
    pl.semaphore_wait(bar, len(partners))

    sends = []

    def block_at(da, db):
        if (da % SIDE, db % SIDE) == (0, 0):
            return blk
        return gbuf.at[c, slot(da, db)]

    def half_copy(n, da, db, axis, by, half):
        na, nb = (da - by, db) if axis == 0 else (da, db - by)
        ta, tb = (by, 0) if axis == 0 else (0, by)
        dz, dy = zy(ta % SIDE, tb % SIDE)
        return pltpu.make_async_remote_copy(
            src_ref=block_at(da, db).at[HALVES[half]],
            dst_ref=gbuf.at[c, slot(na, nb), HALVES[half]],
            send_sem=gsend.at[n],
            recv_sem=grecv.at[slot(na, nb), half],
            device_id=peer(dz, dy),
            device_id_type=MESH,
        )

    def send_half(*what):
        half_copy(len(sends), *what).start()
        sends.append(what)

    def send_full(da, db, axis):
        for by in (1, -1):
            for half in (0, 1):
                send_half(da, db, axis, by, half)

    sib_copies = []

    def sibling_copy(n, da, db):
        return pltpu.make_async_remote_copy(
            src_ref=block_at(da, db),
            dst_ref=gbuf.at[c, slot(da, db)],
            send_sem=bsend.at[n],
            recv_sem=brecv.at[slot(da, db)],
            device_id=sibling,
            device_id_type=MESH,
        )

    def send_sibling(*what):
        sibling_copy(len(sib_copies), *what).start()
        sib_copies.append(what)

    def wait_half(da, db, half):
        ref = gbuf.at[c, slot(da, db), HALVES[half]]
        pltpu.make_async_copy(ref, ref, grecv.at[slot(da, db), half]).wait()

    def arrived(da, db):
        wait_half(da, db, 0)
        wait_half(da, db, 1)
        if db == 0:
            if da == 3:
                send_half(da, db, 0, 1, 0)
            if da == 1:
                send_half(da, db, 0, -1, 1)
            send_full(da, db, 1)
        elif db == 3:
            send_half(da, db, 1, 1, 0)
        elif db == 1:
            send_half(da, db, 1, -1, 1)
        send_sibling(da, db)

    send_sibling(0, 0)
    send_full(0, 0, 0)
    send_full(0, 0, 1)

    cnt[...] = jnp.zeros_like(cnt)
    for cp in wcopies:
        cp.wait()

    row_i = lax.broadcasted_iota(jnp.int32, (TOK, TOK), 0)
    col_i = lax.broadcasted_iota(jnp.int32, (TOK, TOK), 1)
    upper = (row_i < col_i).astype(BF)
    slot_iota = lax.broadcasted_iota(jnp.int32, (ROWS, TOK), 0).astype(F32)

    def routing(ext, expert, core):
        hit = (ext[0:TOP] == expert).astype(F32)
        mask = jnp.sum(hit, axis=0, keepdims=True)
        scale = jnp.sum(hit * ext[TOP : 2 * TOP], axis=0, keepdims=True)
        rank = dot(jnp.broadcast_to(mask, (16, TOK)).astype(BF), upper, 1, 0)[0:1]
        key = jnp.where(mask > 0.5, rank + float(CAP * core), -1.0)
        return (slot_iota == key).astype(F32), scale

    def remote_x(src, dst, ssem, rsem, to):
        return pltpu.make_async_remote_copy(
            src_ref=src, dst_ref=dst, send_sem=ssem, recv_sem=rsem, device_id=(e, to), device_id_type=MESH
        )

    def rs1(t, h):
        return remote_x(
            part.at[lax.rem(t, 3), 1, h], r1.at[t, h], r1s.at[t, h], r1r.at[t, h], (right, left)[h]
        )

    def rs2(t, side):
        return remote_x(
            part.at[lax.rem(t, 3), 2 * side], r2.at[t, side], r2s.at[t, side], r2r.at[t, side], (right, left)[side]
        )

    def ag1(t, side):
        mine = pl.ds(2 * x, 2)
        return remote_x(
            ag.at[t, mine], ag.at[t, mine], a1s.at[t, side], a1r.at[t, side], (right, left)[side]
        )

    def ag1_wait(t, side):
        ref = ag.at[t, pl.ds(2 * (left, right)[side], 2)]
        pltpu.make_async_copy(ref, ref, a1r.at[t, side]).wait()

    def ag2(t, side):
        ref = ag.at[t, 2 * (left, right)[side] + side]
        return remote_x(ref, ref, a2s.at[t, side], a2r.at[t, side], (right, left)[side])

    def ag2_wait(t, side):
        ref = ag.at[t, 2 * lax.rem(x + 2, SIDE) + side]
        pltpu.make_async_copy(ref, ref, a2r.at[t, side]).wait()

    def ret_copy(k):
        dz, dy = ORDER[k]
        if (dz, dy) == (0, 0):
            return pltpu.make_async_copy(rets.at[k], retr.at[chip], rtr.at[chip])
        return pltpu.make_async_remote_copy(
            src_ref=rets.at[k], dst_ref=retr.at[chip], send_sem=rts.at[k], recv_sem=rtr.at[chip],
            device_id=peer(dz, dy), device_id_type=MESH,
        )

    def forward(s):
        for k in range(CHUNKS):

            @pl.when(s == k)
            def _():
                for ev in EVENTS[k]:
                    arrived(*ev)
                loads = []
                for i in range(GROUP):
                    dz, dy = ORDER[k * GROUP + i]
                    at = dz * SIDE + dy
                    ref = gbuf.at[1 - c, at]
                    pltpu.make_async_copy(ref, ref, brecv.at[at]).wait()
                    mine = blk if at == 0 else gbuf.at[c, at]
                    loads.append(pltpu.make_async_copy(mine, stage.at[i, c], stsem.at[2 * i]))
                    loads.append(pltpu.make_async_copy(ref, stage.at[i, 1 - c], stsem.at[2 * i + 1]))
                for cp in loads:
                    cp.start()
                for cp in loads:
                    cp.wait()

        expert = e.astype(F32)
        for i in range(GROUP):
            picks, scales = [], []
            for core in range(2):
                ext = stage[i, core, pl.ds(2 * TOK, 16), pl.ds(0, 2 * TOK)].astype(F32)
                cnt[...] += ext[:, TOK:]
                pick, scale = routing(ext[:, :TOK], expert, core)
                picks.append(pick)
                scales.append(jnp.sum(pick * scale, axis=1, keepdims=True))
            pick = jnp.concatenate(picks, axis=1).astype(BF)
            rows = pl.ds(pl.multiple_of(s * R + i * ROWS, 16), ROWS)
            scl[s, pl.ds(i * ROWS, ROWS), :] = jnp.broadcast_to(scales[0] + scales[1], (ROWS, HID))
            act = jnp.concatenate([stage[i, 0, pl.ds(0, TOK), :], stage[i, 1, pl.ds(0, TOK), :]], axis=0)
            rowact[pl.ds(i * ROWS, ROWS), :] = dot(pick, act, 1, 0).astype(BF)
            cot = jnp.concatenate([stage[i, 0, pl.ds(TOK, TOK), :], stage[i, 1, pl.ds(TOK, TOK), :]], axis=0)
            rowcot[rows, :] = dot(pick, cot, 1, 0).astype(BF)

        at = lax.rem(s, 3)

        @pl.when(s >= 3)
        def _():
            for h in range(2):
                rs1(s - 3, h).wait_send()
                rs2(s - 3, h).wait_send()

        chunk_rows = pl.ds(pl.multiple_of(s * R, 16), R)
        for j in (2, 1, 3, 0):
            a = lax.rem(x + j, SIDE)
            gu = dot(rowact[...], wgu[:, pl.ds(pl.multiple_of(a * 512, 512), 512)], 1, 0)
            d = dot(rowcot[chunk_rows, :], wd[pl.ds(pl.multiple_of(a * 256, 256), 256), :], 1, 1)
            for h in range(2):
                gu_h = gu[:, 256 * h : 256 * h + 256]
                d_h = d[:, HID * h : HID * h + HID]
                if j == 0:
                    own[at, h, :, pl.ds(0, 256)] = gu_h
                    own[at, h, :, pl.ds(256, HID)] = d_h
                else:
                    part[at, j - 1, h, :, pl.ds(0, 256)] = gu_h.astype(BF)
                    part[at, j - 1, h, :, pl.ds(256, HID)] = d_h.astype(BF)
            if j == 2:
                rs1(s, 0).start()
                rs1(s, 1).start()

    def pass_sums(t):
        at = lax.rem(t, 3)
        for h in range(2):
            rs1(t, h).wait_recv()
            part[at, 2 * h, h] = (part[at, 2 * h, h].astype(F32) + r1[t, h].astype(F32)).astype(BF)
            rs2(t, h).start()

    def pointwise(t):
        at = lax.rem(t, 3)
        rs2(t, 0).wait_recv()
        rs2(t, 1).wait_recv()
        scale = scl[t]
        for h in range(2):
            v = own[at, h] + r2[t, 0, h].astype(F32) + r2[t, 1, h].astype(F32)
            gate, up, down = v[:, :HID], v[:, HID : 2 * HID], v[:, 2 * HID :]
            sig = jax.nn.sigmoid(gate)
            act = gate * sig
            slope = sig * (1.0 + gate * (1.0 - sig))
            dh = down * scale
            g = 2 * x + h
            ag[t, g, :, pl.ds(0, HID)] = (dh * up * slope).astype(BF)
            ag[t, g, :, pl.ds(HID, HID)] = (dh * act).astype(BF)
            ag[t, g, :, pl.ds(2 * HID, HID)] = (act * up * scale).astype(BF)
        ag1(t, 0).start()
        ag1(t, 1).start()

    def pass_shares(t):
        for side in range(2):
            ag1_wait(t, side)
            ag2(t, side).start()

    def backward(t):
        ag2_wait(t, 0)
        ag2_wait(t, 1)
        rows = pl.ds(pl.multiple_of(t * R, 16), R)
        for g in range(8):
            hs[rows, pl.ds(g * HID, HID)] = ag[t, g, :, pl.ds(2 * HID, HID)]
        grads = jnp.concatenate([ag[t, g, :, pl.ds(0, 2 * HID)] for g in range(8)], axis=1)
        out = dot(grads, wgu[...], 1, 1).astype(BF)
        for i in range(GROUP):
            rets[t * GROUP + i] = out[i * ROWS : (i + 1) * ROWS]
        for k in range(CHUNKS):

            @pl.when(t == k)
            def _():
                for i in range(GROUP):
                    ret_copy(k * GROUP + i).start()

    def step(s, carry):
        @pl.when((s >= 1) & (s < CHUNKS + 1))
        def _():
            pass_sums(s - 1)

        @pl.when((s >= 2) & (s < CHUNKS + 2))
        def _():
            pointwise(s - 2)

        @pl.when((s >= 3) & (s < CHUNKS + 3))
        def _():
            pass_shares(s - 3)

        @pl.when(s < CHUNKS)
        def _():
            forward(s)

        @pl.when(s >= 4)
        def _():
            backward(s - 4)

        return carry

    lax.fori_loop(0, CHUNKS + 4, step, 0)

    factor = float(2 * CHIPS * TOK) / cnt[0:1, 0:1]
    outs = []
    for f in range(4):
        if f >= 2:
            outs[f - 2].wait()
        dgt[f % 2] = (dot(hs[:, pl.ds(256 * f, 256)], rowcot[...], 0, 0) * factor).astype(BF)
        cp = pltpu.make_async_copy(dgt.at[f % 2], down_grad.at[0, pl.ds(256 * f, 256), :], osem.at[f % 2])
        cp.start()
        outs.append(cp)

    for core in range(2):
        src = stage.at[0, core, pl.ds(2 * TOK, 16), :]

        @pl.when(c == core)
        def _():
            cp = pltpu.make_async_copy(blk.at[pl.ds(2 * TOK, 16)], src, stsem.at[0])
            cp.start()
            cp.wait()

        @pl.when(c != core)
        def _():
            cp = pltpu.make_async_copy(gbuf.at[1 - c, 0, pl.ds(2 * TOK, 16)], src, stsem.at[0])
            cp.start()
            cp.wait()

    for q in range(CHIPS):
        expert = (2 * q + c).astype(F32)
        for core in range(2):
            ext = stage[0, core, pl.ds(2 * TOK, 16), pl.ds(0, TOK)].astype(F32)
            pick, _ = routing(ext, expert, core)
            sall[pl.ds(q * ROWS, ROWS), pl.ds(core * TOK, TOK)] = pick.astype(BF)
    for dz in range(SIDE):
        for dy in range(SIDE):
            ref = retr.at[chip_at(dz, dy)]
            pltpu.make_async_copy(ref, ref, rtr.at[chip_at(dz, dy)]).wait()
    dense[...] = dot(sall[...], retr[...].reshape(CHIPS * ROWS, width), 0, 0)
    swap = pltpu.make_async_remote_copy(
        src_ref=dense.at[pl.ds(pl.multiple_of((1 - c) * TOK, TOK), TOK)],
        dst_ref=sibr,
        send_sem=css.at[0],
        recv_sem=csr.at[0],
        device_id=sibling,
        device_id_type=MESH,
    )
    swap.start()
    swap.wait()
    mine = dense[pl.ds(pl.multiple_of(c * TOK, TOK), TOK), :]
    igt[...] = ((mine + sibr[...]) * factor).astype(BF)
    final = pltpu.make_async_copy(igt, in_grad, osem.at[2])
    final.start()

    final.wait()
    outs[2].wait()
    outs[3].wait()
    for n, what in enumerate(sends):
        half_copy(n, *what).wait_send()
    for n, what in enumerate(sib_copies):
        sibling_copy(n, *what).wait_send()
    for k in range(1, CHIPS):
        ret_copy(k).wait_send()

    def drain(t, carry):
        for h in range(2):
            @pl.when(t >= CHUNKS - 3)
            def _():
                rs1(t, h).wait_send()
                rs2(t, h).wait_send()

            ag1(t, h).wait_send()
            ag2(t, h).wait_send()
        return carry

    lax.fori_loop(0, CHUNKS, drain, 0)


def local(
    activations, cotangent, expert_ids, combine, log_ratio, valid_mask, segment_ids, w_gate, w_up, w_down
):
    tok_rows, width = activations.shape
    groups = lax.axis_size("expert")
    me = lax.axis_index("expert")
    last = jnp.where(me == groups - 1, -1, segment_ids[-1:])
    following = jnp.concatenate([segment_ids[1:], last])
    live = jnp.maximum(valid_mask, (following != segment_ids).astype(jnp.int32)).astype(F32)
    weight = jnp.minimum(jnp.exp(log_ratio), 2.0) * live
    slot_scale = (combine * weight[:, None]).astype(BF)
    routing = jnp.concatenate([expert_ids.T.astype(BF), slot_scale.T], axis=0)
    count = jnp.broadcast_to(jnp.sum(live).astype(BF), (2 * TOP, TOK))
    ext = jnp.concatenate([routing, count, jnp.zeros((2 * TOP, width - 2 * TOK), BF)], axis=1)
    blk = jnp.concatenate([activations, cotangent, ext], axis=0)

    any_spec = pl.BlockSpec(memory_space=pl.ANY)
    dma = pltpu.SemaphoreType.DMA
    in_grad, down_grad, _ = pl.pallas_call(
        kernel,
        out_shape=(
            jax.ShapeDtypeStruct((tok_rows, width), BF),
            jax.ShapeDtypeStruct(w_down.shape, BF),
            jax.ShapeDtypeStruct((2, CHIPS, BLOCK, width), BF),
        ),
        in_specs=[any_spec] * 4,
        out_specs=(any_spec,) * 3,
        scratch_shapes=[
            pltpu.VMEM((width, 2048), BF),
            pltpu.VMEM((1024, width), BF),
            pltpu.VMEM((GROUP, 2, BLOCK, width), BF),
            pltpu.VMEM((R, width), BF),
            pltpu.VMEM((CHIPS * ROWS, width), BF),
            pltpu.VMEM((CHUNKS, R, HID), F32),
            pltpu.VMEM((3, 3, 2, R, 3 * HID), BF),
            pltpu.VMEM((3, 2, R, 3 * HID), F32),
            pltpu.VMEM((CHUNKS, 2, R, 3 * HID), BF),
            pltpu.VMEM((CHUNKS, 2, 2, R, 3 * HID), BF),
            pltpu.VMEM((CHUNKS, 8, R, 3 * HID), BF),
            pltpu.VMEM((CHIPS * ROWS, 1024), BF),
            pltpu.VMEM((CHIPS, ROWS, width), BF),
            pltpu.VMEM((CHIPS, ROWS, width), BF),
            pltpu.VMEM((2 * TOK, width), F32),
            pltpu.VMEM((TOK, width), F32),
            pltpu.VMEM((CHIPS * ROWS, 2 * TOK), BF),
            pltpu.VMEM((2, 256, width), BF),
            pltpu.VMEM((TOK, width), BF),
            pltpu.VMEM((16, TOK), F32),
            dma((17,)), dma((2 * GROUP,)),
            dma((26 * 2,)), dma((CHIPS, 2)), dma((CHIPS,)), dma((CHIPS,)),
            dma((CHUNKS, 2)), dma((CHUNKS, 2)), dma((CHUNKS, 2)), dma((CHUNKS, 2)),
            dma((CHUNKS, 2)), dma((CHUNKS, 2)), dma((CHUNKS, 2)), dma((CHUNKS, 2)),
            dma((CHIPS,)), dma((CHIPS,)), dma((1,)), dma((1,)), dma((3,)),
        ],
        compiler_params=pltpu.CompilerParams(
            collective_id=0, has_side_effects=True, vmem_limit_bytes=63 * 2**20
        ),
        cost_estimate=pl.CostEstimate(flops=28_200_000_000, bytes_accessed=60_000_000, transcendentals=1_000_000),
    )(blk, w_gate, w_up, w_down)
    return in_grad, down_grad


def solution(mesh):
    return jax.shard_map(
        local,
        mesh=mesh,
        in_specs=(
            P("expert", "tensor"),
            P("expert", "tensor"),
            P("expert", None),
            P("expert", None),
            P("expert"),
            P("expert"),
            P("expert"),
            P("expert", "tensor", None),
            P("expert", "tensor", None),
            P("expert", None, "tensor"),
        ),
        out_specs=(P("expert", "tensor"), P("expert", None, "tensor")),
        check_vma=False,
    )
```

time: 658 us -> 230 us (0.35)
  the two profiles are of different devices: /device:TPU:0 before, /device:TPU:75 now
where the time goes in v1:
time: 230 us
  Pallas kernels  215 us (93%)
  local copies, waits for them, and re-layouts  8.55 us (4%)
  other arithmetic  4.91 us (2%)
    pallas_call x1, Pallas kernels, local(): pl.pallas_call(kernel, out_shape=(jax.ShapeDtypeStruct((tok_rows, width),...  215 us
    unnamed x2, local copies, waits for them, and re-layouts  5.93 us

profile of v1, /device:TPU:75, one launch (start us, length us, event | category | flops | bytes accessed | tf_op | source)
XLA Modules:
  0.0 229.6 jit_solution(4059376672133348232)
XLA Ops:
  0.6 1.2 slice.7
  2.5 0.7 slice.6
  3.3 0.8 minimum_multiply_fusion
  4.0 0.6 reduce_sum.9
  4.6 0.7 fusion
  5.3 0.7 convert_bitcast_fusion
  6.0 0.6 broadcast_in_dim.9
  6.7 2.2 maximum_maximum_fusion.blk
  8.8 214.9 %shard_map.113 = (bf16[128,1792]{1,0:T(8,128)(2,1)}, bf16[1,1024,1792]{2,1,0:T(8,128)(2,1)}, bf16[2,16,272,1792]{3,2,1,0:T(8,128)(2,1)}) custom-call(bf16[272,1792]{1,0:T(8,128)(2,1)} %maximum_maximum_fusion.blk, bf16[1,1792,1024]{2,1,0:T(8,128)(2,1)} %w_gate.1, bf16[1,1792,1024]{2,1,0:T(8,128)(2,1)} %w_up.1, bf16[1,1024,1792]{2,1,0:T(8,128)(2,1)} %w_down.1), custom_call_target="tpu_custom_call" | custom-call | flops 28199999488 | bytes 60000000 | tf_op jit(solution)/shard_map/pallas_call | solution.py:457
  223.7 1.8 copy.14
  225.5 4.1 %copy.15 = bf16[1,1024,1792]{2,1,0:T(8,128)(2,1)} copy(bf16[1,1024,1792]{2,1,0:T(8,128)(2,1)} %get-tuple-element.11) | data formatting | bytes 7340032
  (1 shorter events, 0.0 us)

commit v2 on v1

v2 whole, which is shorter than its diff:
```python
import functools

import jax
import jax.numpy as jnp
from jax import lax
from jax.experimental import pallas as pl
from jax.experimental.pallas import tpu as pltpu
from jax.sharding import PartitionSpec as P

BF = jnp.bfloat16
F32 = jnp.float32
MESH = pl.DeviceIdType.MESH

SIDE = 4
CHIPS = SIDE * SIDE
CAP = 40
TOK = 128
ROWS = 2 * CAP
TOP = 8
HID = 128
LANES = 3 * HID
BLOCK = 2 * TOK + 16
LAST = 8

ORDER = [
    (0, 0),
    (3, 0), (1, 0),
    (0, 3), (0, 1),
    (3, 3), (3, 1),
    (2, 3), (3, 2),
    (2, 2), (2, 1),
    (1, 2), (1, 3),
    (2, 0), (0, 2),
    (1, 1),
]
CHUNK = [ORDER[:1]] + [ORDER[i : i + 2] for i in range(1, 15, 2)] + [ORDER[15:]]
BEFORE = {
    1: [("wait", (3, 0)), ("wait", (1, 0)), ("full", (0, 0), 1)],
    2: [("wait", (0, 3)), ("wait", (0, 1))],
    3: [("wait", (3, 3)), ("wait", (3, 1)), ("half", (3, 3), 1, 1, 0), ("half", (3, 1), 1, -1, 1)],
    4: [
        ("wait", (2, 3)), ("wait", (2, 1)), ("half", (2, 3), 1, 1, 0), ("half", (2, 1), 1, -1, 1),
        ("wait", (3, 2)),
    ],
    5: [("wait", (2, 2))],
    6: [("wait", (1, 2)), ("wait", (0, 2))],
}
AFTER = {
    1: [("half", (3, 0), 0, 1, 0), ("half", (1, 0), 0, -1, 1), ("full", (3, 0), 1)],
    2: [("wait", (2, 0)), ("full", (2, 0), 1)],
    3: [("full", (1, 0), 1)],
    4: [("half", (0, 3), 1, 1, 0), ("half", (0, 1), 1, -1, 1)],
    5: [("wait", (1, 3)), ("wait", (1, 1)), ("half", (1, 3), 1, 1, 0), ("half", (1, 1), 1, -1, 1)],
}
HALVES = (pl.ds(0, TOK), pl.ds(TOK, BLOCK - TOK))


def first_of(t):
    return max(2 * t - 1, 0) if isinstance(t, int) else 2 * t - lax.div(t + 8, 9)


def dot(a, b, ca, cb):
    return lax.dot_general(a, b, (((ca,), (cb,)), ((), ())), preferred_element_type=F32)


def kernel(
    acts, cots, ids, combine, log_ratio, valid, segments, w_gate, w_up, w_down,
    in_grad, down_grad, gbuf,
    wgu, wd, mine, stage, rowact, rowcot, scl, part, own, r1, r2, ag, hs, rets, retr, dense, sibr, sall,
    dgt, igt, cnt,
    wsem, stsem, gsend, grecv, bsend, brecv, r1s, r1r, r2s, r2r, a1s, a1r, a2s, a2r, rts, rtr,
    css, csr, osem,
):
    e = lax.axis_index("expert")
    x = lax.axis_index("tensor")
    c = lax.rem(e, 2)
    chip = lax.div(e, 2)
    z = lax.div(chip, SIDE)
    y = lax.rem(chip, SIDE)
    width = acts.shape[1]
    right = lax.rem(x + 1, SIDE)
    left = lax.rem(x + SIDE - 1, SIDE)

    def chip_at(dz, dy):
        return lax.rem(z + dz, SIDE) * SIDE + lax.rem(y + dy, SIDE)

    def peer(dz, dy):
        return (chip_at(dz, dy) * 2 + c, x)

    sibling = (chip * 2 + 1 - c, x)

    def zy(da, db):
        return da * (1 - c) + db * c, da * c + db * (1 - c)

    def slot(da, db):
        dz, dy = zy(da % SIDE, db % SIDE)
        return dz * SIDE + dy

    bar = pltpu.get_barrier_semaphore()
    partners = [(e, right), (e, left), sibling]
    partners += [peer(dz, dy) for dz in range(SIDE) for dy in range(SIDE) if (dz, dy) != (0, 0)]
    for p in partners:
        pl.semaphore_signal(bar, inc=1, device_id=p, device_id_type=MESH)

    wcopies = []
    for g in range(8):
        cols = pl.ds(g * HID, HID)
        wcopies.append(
            pltpu.make_async_copy(w_gate.at[0, :, cols], wgu.at[:, pl.ds(2 * g * HID, HID)], wsem.at[2 * g])
        )
        wcopies.append(
            pltpu.make_async_copy(w_up.at[0, :, cols], wgu.at[:, pl.ds((2 * g + 1) * HID, HID)], wsem.at[2 * g + 1])
        )
    wcopies.append(pltpu.make_async_copy(w_down.at[0], wd, wsem.at[16]))
    loads = [
        pltpu.make_async_copy(acts, mine.at[pl.ds(0, TOK)], stsem.at[0]),
        pltpu.make_async_copy(cots, mine.at[pl.ds(TOK, TOK)], stsem.at[1]),
    ]
    for cp in loads + wcopies:
        cp.start()

    lane = lax.broadcasted_iota(jnp.int32, (TOP, TOK), 1)
    seg = jnp.broadcast_to(segments[...], (TOP, TOK))
    following = pltpu.roll(seg, TOK - 1, 1)
    final_dev = (e + 1) // (2 * CHIPS)
    closing = jnp.where(lane == TOK - 1, final_dev, (following != seg).astype(jnp.int32))
    live = jnp.maximum(jnp.broadcast_to(valid[...], (TOP, TOK)), closing).astype(F32)
    weight = jnp.minimum(jnp.exp(jnp.broadcast_to(log_ratio[...], (TOP, TOK))), 2.0) * live
    slot_scale = (combine[...].T * weight).astype(BF)
    count = jnp.broadcast_to(jnp.sum(live, axis=1, keepdims=True), (TOP, TOK)).astype(BF)
    tail = pl.ds(2 * TOK, 2 * TOP)
    mine[tail, :] = jnp.zeros((2 * TOP, width), BF)
    mine[tail, pl.ds(0, TOK)] = jnp.concatenate([ids[...].astype(F32).T.astype(BF), slot_scale], axis=0)
    mine[tail, pl.ds(TOK, TOK)] = jnp.concatenate([count, count], axis=0)
    for cp in loads:
        cp.wait()
    pl.semaphore_wait(bar, len(partners))

    sends = []

    def block_at(da, db):
        if (da % SIDE, db % SIDE) == (0, 0):
            return mine
        return gbuf.at[c, slot(da, db)]

    def half_copy(n, da, db, axis, by, half):
        na, nb = (da - by, db) if axis == 0 else (da, db - by)
        ta, tb = (by, 0) if axis == 0 else (0, by)
        dz, dy = zy(ta % SIDE, tb % SIDE)
        return pltpu.make_async_remote_copy(
            src_ref=block_at(da, db).at[HALVES[half]],
            dst_ref=gbuf.at[c, slot(na, nb), HALVES[half]],
            send_sem=gsend.at[n],
            recv_sem=grecv.at[slot(na, nb), half],
            device_id=peer(dz, dy),
            device_id_type=MESH,
        )

    def send_half(*what):
        half_copy(len(sends), *what).start()
        sends.append(what)

    def send_full(da, db, axis):
        for by in (1, -1):
            for half in (0, 1):
                send_half(da, db, axis, by, half)

    sib_copies = []

    def sibling_copy(n, da, db):
        return pltpu.make_async_remote_copy(
            src_ref=block_at(da, db),
            dst_ref=gbuf.at[c, slot(da, db)],
            send_sem=bsend.at[n],
            recv_sem=brecv.at[slot(da, db)],
            device_id=sibling,
            device_id_type=MESH,
        )

    def send_sibling(*what):
        sibling_copy(len(sib_copies), *what).start()
        sib_copies.append(what)

    def wait_half(da, db, half):
        ref = gbuf.at[c, slot(da, db), HALVES[half]]
        pltpu.make_async_copy(ref, ref, grecv.at[slot(da, db), half]).wait()

    def act_on(events):
        for kind, at, *rest in events:
            if kind == "wait":
                wait_half(*at, 0)
                wait_half(*at, 1)
                send_sibling(*at)
            elif kind == "full":
                send_full(*at, *rest)
            else:
                send_half(*at, *rest)

    send_sibling(0, 0)
    send_full(0, 0, 0)

    cnt[...] = jnp.zeros_like(cnt)

    row_i = lax.broadcasted_iota(jnp.int32, (TOK, TOK), 0)
    col_i = lax.broadcasted_iota(jnp.int32, (TOK, TOK), 1)
    upper = (row_i < col_i).astype(BF)
    slot_iota = lax.broadcasted_iota(jnp.int32, (ROWS, TOK), 0).astype(F32)

    def routing(ext, expert, core):
        hit = (ext[0:TOP] == expert).astype(F32)
        mask = jnp.sum(hit, axis=0, keepdims=True)
        scale = jnp.sum(hit * ext[TOP : 2 * TOP], axis=0, keepdims=True)
        rank = dot(jnp.broadcast_to(mask, (16, TOK)).astype(BF), upper, 1, 0)[0:1]
        key = jnp.where(mask > 0.5, rank + float(CAP * core), -1.0)
        return (slot_iota == key).astype(F32), scale

    def remote_x(src, dst, ssem, rsem, to):
        return pltpu.make_async_remote_copy(
            src_ref=src, dst_ref=dst, send_sem=ssem, recv_sem=rsem, device_id=(e, to), device_id_type=MESH
        )

    def rs1(t, n, h):
        return remote_x(
            part.at[lax.rem(t, 3), pl.ds(0, n), 1, h], r1.at[pl.ds(first_of(t), n), h],
            r1s.at[t, h], r1r.at[t, h], (right, left)[h],
        )

    def rs2(t, n, side):
        return remote_x(
            part.at[lax.rem(t, 3), pl.ds(0, n), 2 * side], r2.at[pl.ds(first_of(t), n), side],
            r2s.at[t, side], r2r.at[t, side], (right, left)[side],
        )

    def ag1(t, n, side):
        ref = ag.at[pl.ds(first_of(t), n), pl.ds(2 * x, 2)]
        return remote_x(ref, ref, a1s.at[t, side], a1r.at[t, side], (right, left)[side])

    def ag1_wait(t, n, side):
        ref = ag.at[pl.ds(first_of(t), n), pl.ds(2 * (left, right)[side], 2)]
        pltpu.make_async_copy(ref, ref, a1r.at[t, side]).wait()

    def ag2(t, n, side):
        ref = ag.at[pl.ds(first_of(t), n), 2 * (left, right)[side] + side]
        return remote_x(ref, ref, a2s.at[t, side], a2r.at[t, side], (right, left)[side])

    def ag2_wait(t, n, side):
        ref = ag.at[pl.ds(first_of(t), n), 2 * lax.rem(x + 2, SIDE) + side]
        pltpu.make_async_copy(ref, ref, a2r.at[t, side]).wait()

    def ret_copy(k):
        dz, dy = ORDER[k]
        if k == 0:
            return pltpu.make_async_copy(rets.at[0], retr.at[0], rtr.at[0])
        return pltpu.make_async_remote_copy(
            src_ref=rets.at[k], dst_ref=retr.at[k], send_sem=rts.at[k], recv_sem=rtr.at[k],
            device_id=peer(dz, dy), device_id_type=MESH,
        )

    def load_stage(elements):
        copies = []
        for i, at in enumerate(elements):
            da, db = at
            theirs = (da * c + db * (1 - c)) * SIDE + da * (1 - c) + db * c
            ref = gbuf.at[1 - c, theirs]
            pltpu.make_async_copy(ref, ref, brecv.at[theirs]).wait()
            copies.append(pltpu.make_async_copy(block_at(*at), stage.at[i, c], stsem.at[2 * i]))
            copies.append(pltpu.make_async_copy(ref, stage.at[i, 1 - c], stsem.at[2 * i + 1]))
        for cp in copies:
            cp.start()
        for cp in copies:
            cp.wait()

    def sends_done(t, n):
        for h in range(2):
            rs1(t, n, h).wait_send()
            rs2(t, n, h).wait_send()

    def forward(t, n):
        first = first_of(t)
        expert = e.astype(F32)
        for i in range(n):
            picks, scales = [], []
            for core in range(2):
                ext = stage[i, core, pl.ds(2 * TOK, 16), pl.ds(0, 2 * TOK)].astype(F32)
                cnt[...] += ext[:, TOK:]
                pick, scale = routing(ext[:, :TOK], expert, core)
                picks.append(pick)
                scales.append(jnp.sum(pick * scale, axis=1, keepdims=True))
            pick = jnp.concatenate(picks, axis=1).astype(BF)
            rows = pl.ds(pl.multiple_of((first + i) * ROWS, 16), ROWS)
            scl[first + i] = jnp.broadcast_to(scales[0] + scales[1], (ROWS, HID))
            act = jnp.concatenate([stage[i, 0, pl.ds(0, TOK), :], stage[i, 1, pl.ds(0, TOK), :]], axis=0)
            rowact[pl.ds(i * ROWS, ROWS), :] = dot(pick, act, 1, 0).astype(BF)
            cot = jnp.concatenate([stage[i, 0, pl.ds(TOK, TOK), :], stage[i, 1, pl.ds(TOK, TOK), :]], axis=0)
            rowcot[rows, :] = dot(pick, cot, 1, 0).astype(BF)

        at = lax.rem(t, 3)
        chunk_rows = pl.ds(pl.multiple_of(first * ROWS, 16), n * ROWS)
        for j in (2, 1, 3, 0):
            a = lax.rem(x + j, SIDE)
            gu = dot(rowact[pl.ds(0, n * ROWS), :], wgu[:, pl.ds(pl.multiple_of(a * 512, 512), 512)], 1, 0)
            d = dot(rowcot[chunk_rows, :], wd[pl.ds(pl.multiple_of(a * 256, 256), 256), :], 1, 1)
            for i in range(n):
                for h in range(2):
                    gu_h = gu[i * ROWS : (i + 1) * ROWS, 256 * h : 256 * h + 256]
                    d_h = d[i * ROWS : (i + 1) * ROWS, HID * h : HID * h + HID]
                    if j == 0:
                        own[at, i, h, :, pl.ds(0, 256)] = gu_h
                        own[at, i, h, :, pl.ds(256, HID)] = d_h
                    else:
                        part[at, i, j - 1, h, :, pl.ds(0, 256)] = gu_h.astype(BF)
                        part[at, i, j - 1, h, :, pl.ds(256, HID)] = d_h.astype(BF)
            if j == 2:
                rs1(t, n, 0).start()
                rs1(t, n, 1).start()

    def pass_sums(t, n):
        at = lax.rem(t, 3)
        first = first_of(t)
        for h in range(2):
            rs1(t, n, h).wait_recv()
            for i in range(n):
                part[at, i, 2 * h, h] = (part[at, i, 2 * h, h].astype(F32) + r1[first + i, h].astype(F32)).astype(BF)
            rs2(t, n, h).start()

    def pointwise(t, n):
        at = lax.rem(t, 3)
        first = first_of(t)
        rs2(t, n, 0).wait_recv()
        rs2(t, n, 1).wait_recv()
        for i in range(n):
            scale = scl[first + i]
            for h in range(2):
                v = own[at, i, h] + r2[first + i, 0, h].astype(F32) + r2[first + i, 1, h].astype(F32)
                gate, up, down = v[:, :HID], v[:, HID : 2 * HID], v[:, 2 * HID :]
                sig = jax.nn.sigmoid(gate)
                act = gate * sig
                slope = sig * (1.0 + gate * (1.0 - sig))
                dh = down * scale
                g = 2 * x + h
                ag[first + i, g, :, pl.ds(0, HID)] = (dh * up * slope).astype(BF)
                ag[first + i, g, :, pl.ds(HID, HID)] = (dh * act).astype(BF)
                ag[first + i, g, :, pl.ds(2 * HID, HID)] = (act * up * scale).astype(BF)
        ag1(t, n, 0).start()
        ag1(t, n, 1).start()

    def pass_shares(t, n):
        for side in range(2):
            ag1_wait(t, n, side)
            ag2(t, n, side).start()

    def backward(t, n):
        ag2_wait(t, n, 0)
        ag2_wait(t, n, 1)
        first = first_of(t)
        grads = []
        for i in range(n):
            rows = pl.ds(pl.multiple_of((first + i) * ROWS, 16), ROWS)
            for g in range(8):
                hs[rows, pl.ds(g * HID, HID)] = ag[first + i, g, :, pl.ds(2 * HID, HID)]
            grads.append(jnp.concatenate([ag[first + i, g, :, pl.ds(0, 2 * HID)] for g in range(8)], axis=1))
        grads = jnp.concatenate(grads, axis=0) if n > 1 else grads[0]
        rowact[pl.ds(0, n * ROWS), :] = dot(grads, wgu[...], 1, 1).astype(BF)

        core0 = lax.broadcasted_iota(jnp.int32, (ROWS, width), 0) < CAP
        for k, elements in enumerate(CHUNK):
            if len(elements) != n:
                continue

            @pl.when(t == k)
            def _():
                for i, (da, db) in enumerate(elements):
                    k0, k1 = ORDER.index((da, db)), ORDER.index((db, da))
                    out = rowact[pl.ds(i * ROWS, ROWS), :]
                    if k0 < k1:
                        rets[k0] = out
                        rets[k1] = out
                    elif k0 == k1:
                        rets[k0] = out
                        ret_copy(k0).start()
                    else:
                        wide = out.astype(F32)
                        rets[k0] = jnp.where(core0, wide, rets[k0].astype(F32)).astype(BF)
                        rets[k1] = jnp.where(core0, rets[k1].astype(F32), wide).astype(BF)
                        ret_copy(k0).start()
                        ret_copy(k1).start()

    def on(cond, f, *args):
        @pl.when(cond)
        def _():
            f(*args)

    def any_size(t, f):
        on((t >= 1) & (t < LAST), f, t, 2)
        on(t == LAST, f, t, 1)

    load_stage(CHUNK[0])
    for cp in wcopies:
        cp.wait()
    forward(0, 1)
    for core in range(2):
        ext = stage[0, core, pl.ds(2 * TOK, 16), pl.ds(0, TOK)].astype(F32)
        for k, (dz, dy) in enumerate(ORDER):
            expert = (2 * chip_at(-dz % SIDE, -dy % SIDE) + c).astype(F32)
            pick, _ = routing(ext, expert, core)
            sall[pl.ds(k * ROWS, ROWS), pl.ds(core * TOK, TOK)] = pick.astype(BF)
    pass_sums(0, 1)
    pointwise(0, 1)

    def step(s, carry):
        any_size(s - 1, pass_sums)
        any_size(s - 2, pointwise)
        for k in range(1, LAST + 1):

            @pl.when(s == k)
            def _():
                act_on(BEFORE.get(k, []))
                load_stage(CHUNK[k])

        on(s == 3, sends_done, 0, 1)
        on((s >= 4) & (s <= LAST), sends_done, s - 3, 2)
        any_size(s, forward)
        for k in AFTER:

            @pl.when(s == k)
            def _():
                act_on(AFTER[k])

        on(s == 1, pass_shares, 0, 1)
        any_size(s - 2, pass_shares)
        t = s - 3
        on((t >= 1) & (t < LAST), backward, t, 2)
        on((t == 0) | (t == LAST), backward, t, 1)
        return carry

    lax.fori_loop(1, LAST + 4, step, 0)

    factor = float(2 * CHIPS * TOK) / cnt[0:1, 0:1]
    outs = []
    for f in range(4):
        if f >= 2:
            outs[f - 2].wait()
        dgt[f % 2] = (dot(hs[:, pl.ds(256 * f, 256)], rowcot[...], 0, 0) * factor).astype(BF)
        cp = pltpu.make_async_copy(dgt.at[f % 2], down_grad.at[0, pl.ds(256 * f, 256), :], osem.at[f % 2])
        cp.start()
        outs.append(cp)

    for k in range(CHIPS):
        pltpu.make_async_copy(retr.at[k], retr.at[k], rtr.at[k]).wait()
    dense[...] = dot(sall[...], retr[...].reshape(CHIPS * ROWS, width), 0, 0)
    swap = pltpu.make_async_remote_copy(
        src_ref=dense.at[pl.ds(pl.multiple_of((1 - c) * TOK, TOK), TOK)],
        dst_ref=sibr,
        send_sem=css.at[0],
        recv_sem=csr.at[0],
        device_id=sibling,
        device_id_type=MESH,
    )
    swap.start()
    swap.wait()
    kept = dense[pl.ds(pl.multiple_of(c * TOK, TOK), TOK), :]
    igt[...] = ((kept + sibr[...]) * factor).astype(BF)
    final = pltpu.make_async_copy(igt, in_grad, osem.at[2])
    final.start()

    final.wait()
    outs[2].wait()
    outs[3].wait()
    for n, what in enumerate(sends):
        half_copy(n, *what).wait_send()
    for n, what in enumerate(sib_copies):
        sibling_copy(n, *what).wait_send()
    for k in range(1, CHIPS):
        ret_copy(k).wait_send()

    for t in (6, 7):
        sends_done(t, 2)
    sends_done(LAST, 1)

    def drain(t, n):
        for h in range(2):
            ag1(t, n, h).wait_send()
            ag2(t, n, h).wait_send()

    def drain_pair(t, carry):
        drain(t, 2)
        return carry

    drain(0, 1)
    lax.fori_loop(1, LAST, drain_pair, 0)
    drain(LAST, 1)


def local(
    activations, cotangent, expert_ids, combine, log_ratio, valid_mask, segment_ids, w_gate, w_up, w_down
):
    tok_rows, width = activations.shape
    any_spec = pl.BlockSpec(memory_space=pl.ANY)
    dma = pltpu.SemaphoreType.DMA
    in_grad, down_grad, _ = pl.pallas_call(
        kernel,
        out_shape=(
            jax.ShapeDtypeStruct((tok_rows, width), BF),
            jax.ShapeDtypeStruct(w_down.shape, BF),
            jax.ShapeDtypeStruct((2, CHIPS, BLOCK, width), BF),
        ),
        in_specs=[any_spec] * 2 + [pl.BlockSpec(memory_space=pltpu.VMEM)] * 5 + [any_spec] * 3,
        out_specs=(any_spec,) * 3,
        scratch_shapes=[
            pltpu.VMEM((width, 2048), BF),
            pltpu.VMEM((1024, width), BF),
            pltpu.VMEM((BLOCK, width), BF),
            pltpu.VMEM((2, 2, BLOCK, width), BF),
            pltpu.VMEM((2 * ROWS, width), BF),
            pltpu.VMEM((CHIPS * ROWS, width), BF),
            pltpu.VMEM((CHIPS, ROWS, HID), F32),
            pltpu.VMEM((3, 2, 3, 2, ROWS, LANES), BF),
            pltpu.VMEM((3, 2, 2, ROWS, LANES), F32),
            pltpu.VMEM((CHIPS, 2, ROWS, LANES), BF),
            pltpu.VMEM((CHIPS, 2, 2, ROWS, LANES), BF),
            pltpu.VMEM((CHIPS, 8, ROWS, LANES), BF),
            pltpu.VMEM((CHIPS * ROWS, 1024), BF),
            pltpu.VMEM((CHIPS, ROWS, width), BF),
            pltpu.VMEM((CHIPS, ROWS, width), BF),
            pltpu.VMEM((2 * TOK, width), F32),
            pltpu.VMEM((TOK, width), F32),
            pltpu.VMEM((CHIPS * ROWS, 2 * TOK), BF),
            pltpu.VMEM((2, 256, width), BF),
            pltpu.VMEM((TOK, width), BF),
            pltpu.VMEM((16, TOK), F32),
            dma((17,)), dma((4,)),
            dma((26 * 2,)), dma((CHIPS, 2)), dma((CHIPS,)), dma((CHIPS,)),
            dma((LAST + 1, 2)), dma((LAST + 1, 2)), dma((LAST + 1, 2)), dma((LAST + 1, 2)),
            dma((LAST + 1, 2)), dma((LAST + 1, 2)), dma((LAST + 1, 2)), dma((LAST + 1, 2)),
            dma((CHIPS,)), dma((CHIPS,)), dma((1,)), dma((1,)), dma((3,)),
        ],
        compiler_params=pltpu.CompilerParams(
            collective_id=0, has_side_effects=True, vmem_limit_bytes=63 * 2**20
        ),
        cost_estimate=pl.CostEstimate(flops=28_200_000_000, bytes_accessed=60_000_000, transcendentals=1_000_000),
    )(
        activations, cotangent, expert_ids, combine, log_ratio[None], valid_mask[None], segment_ids[None],
        w_gate, w_up, w_down,
    )
    return in_grad, down_grad


def solution(mesh):
    return jax.shard_map(
        local,
        mesh=mesh,
        in_specs=(
            P("expert", "tensor"),
            P("expert", "tensor"),
            P("expert", None),
            P("expert", None),
            P("expert"),
            P("expert"),
            P("expert"),
            P("expert", "tensor", None),
            P("expert", "tensor", None),
            P("expert", None, "tensor"),
        ),
        out_specs=(P("expert", "tensor"), P("expert", None, "tensor")),
        check_vma=False,
    )
```

time: 230 us -> 214 us (0.930)
  the two profiles are of different devices: /device:TPU:75 before, /device:TPU:107 now
where the time goes in v2:
time: 214 us; the launch traced here: 213 us
  Pallas kernels  204 us (95%)
  local copies, waits for them, and re-layouts  8.76 us (4%)
    pallas_call x1, Pallas kernels, local(): pl.pallas_call(kernel, out_shape=(jax.ShapeDtypeStruct((tok_rows, width),...  204 us
    unnamed x4, local copies, waits for them, and re-layouts  8.76 us

profile of v2, /device:TPU:107, one launch (start us, length us, event | category | flops | bytes accessed | tf_op | source)
XLA Modules:
  0.0 213.1 jit_solution(1322131450267907107)
XLA Ops:
  0.6 1.4 copy.12.ids
  2.0 1.4 copy.13.combine
  3.5 203.7 %shard_map.113 = (bf16[128,1792]{1,0:T(8,128)(2,1)}, bf16[1,1024,1792]{2,1,0:T(8,128)(2,1)}, bf16[2,16,272,1792]{3,2,1,0:T(8,128)(2,1)}) custom-call(bf16[128,1792]{1,0:T(8,128)(2,1)} %acts.1, bf16[128,1792]{1,0:T(8,128)(2,1)} %cots.1, s32[128,8]{1,0:T(8,128)} %copy.12.ids, f32[128,8]{1,0:T(8,128)} %copy.13.combine, f32[1,128]{1,0:T(1,128)} %bitcast.3, ...), custom_call_target="tpu_custom_call" | custom-call | flops 28199999488 | bytes 60000000 | tf_op jit(solution)/shard_map/pallas_call | solution.py:500
  207.2 1.8 copy.16
  209.0 4.1 %copy.17 = bf16[1,1024,1792]{2,1,0:T(8,128)(2,1)} copy(bf16[1,1024,1792]{2,1,0:T(8,128)(2,1)} %get-tuple-element.9) | data formatting | bytes 7340032

commit v3 on v2

--- a/solution.py
+++ b/solution.py
@@ -19,38 +19,91 @@
 TOP = 8
 HID = 128
 LANES = 3 * HID
-BLOCK = 2 * TOK + 16
+BLOCK = 2 * TOK
 LAST = 8
 
 ORDER = [
     (0, 0),
-    (3, 0), (1, 0),
-    (0, 3), (0, 1),
+    (1, 0), (3, 0),
+    (0, 1), (0, 3),
+    (1, 3), (1, 1),
     (3, 3), (3, 1),
-    (2, 3), (3, 2),
-    (2, 2), (2, 1),
-    (1, 2), (1, 3),
+    (2, 1), (1, 2),
+    (3, 2), (2, 3),
     (2, 0), (0, 2),
-    (1, 1),
+    (2, 2),
 ]
 CHUNK = [ORDER[:1]] + [ORDER[i : i + 2] for i in range(1, 15, 2)] + [ORDER[15:]]
-BEFORE = {
-    1: [("wait", (3, 0)), ("wait", (1, 0)), ("full", (0, 0), 1)],
-    2: [("wait", (0, 3)), ("wait", (0, 1))],
-    3: [("wait", (3, 3)), ("wait", (3, 1)), ("half", (3, 3), 1, 1, 0), ("half", (3, 1), 1, -1, 1)],
-    4: [
-        ("wait", (2, 3)), ("wait", (2, 1)), ("half", (2, 3), 1, 1, 0), ("half", (2, 1), 1, -1, 1),
+PASS_ON = {
+    (0, "S"): [
+        ("full", (0, 0), 1),
+    ],
+    (0, "P"): [
+        ("wait", (3, 0)),
+        ("wait", (1, 0)),
+    ],
+    (1, "L"): [
+        ("full", (1, 0), 1),
+    ],
+    (1, "F"): [
+        ("wait", (0, 1)),
+        ("half", (3, 0), 0, 1, 0),
+        ("wait", (0, 3)),
+    ],
+    (2, "L"): [
+        ("full", (3, 0), 1),
+    ],
+    (3, "P"): [
+        ("wait", (1, 1)),
+        ("wait", (1, 3)),
+        ("half", (1, 0), 0, -1, 1),
+    ],
+    (3, "B"): [
+        ("half", (1, 1), 1, -1, 1),
+    ],
+    (3, "L"): [
+        ("half", (1, 3), 1, 1, 0),
+    ],
+    (3, "F"): [
+        ("wait", (3, 3)),
+    ],
+    (4, "P"): [
+        ("half", (0, 1), 1, -1, 1),
+        ("wait", (3, 1)),
+        ("wait", (2, 0)),
+    ],
+    (4, "S"): [
+        ("half", (0, 3), 1, 1, 0),
+        ("full", (2, 0), 1),
+    ],
+    (4, "L"): [
+        ("half", (3, 1), 1, -1, 1),
+    ],
+    (4, "F"): [
+        ("wait", (1, 2)),
+    ],
+    (4, "H"): [
+        ("half", (3, 3), 1, 1, 0),
+    ],
+    (5, "P"): [
+        ("wait", (2, 1)),
+    ],
+    (5, "B"): [
         ("wait", (3, 2)),
     ],
-    5: [("wait", (2, 2))],
-    6: [("wait", (1, 2)), ("wait", (0, 2))],
-}
-AFTER = {
-    1: [("half", (3, 0), 0, 1, 0), ("half", (1, 0), 0, -1, 1), ("full", (3, 0), 1)],
-    2: [("wait", (2, 0)), ("full", (2, 0), 1)],
-    3: [("full", (1, 0), 1)],
-    4: [("half", (0, 3), 1, 1, 0), ("half", (0, 1), 1, -1, 1)],
-    5: [("wait", (1, 3)), ("wait", (1, 1)), ("half", (1, 3), 1, 1, 0), ("half", (1, 1), 1, -1, 1)],
+    (5, "L"): [
+        ("half", (2, 1), 1, -1, 1),
+    ],
+    (5, "F"): [
+        ("wait", (2, 3)),
+    ],
+    (6, "F"): [
+        ("half", (2, 3), 1, 1, 0),
+    ],
+    (7, "P"): [
+        ("wait", (2, 2)),
+        ("wait", (0, 2)),
+    ],
 }
 HALVES = (pl.ds(0, TOK), pl.ds(TOK, BLOCK - TOK))
 
@@ -66,9 +119,9 @@
 def kernel(
     acts, cots, ids, combine, log_ratio, valid, segments, w_gate, w_up, w_down,
     in_grad, down_grad, gbuf,
-    wgu, wd, mine, stage, rowact, rowcot, scl, part, own, r1, r2, ag, hs, rets, retr, dense, sibr, sall,
-    dgt, igt, cnt,
-    wsem, stsem, gsend, grecv, bsend, brecv, r1s, r1r, r2s, r2r, a1s, a1r, a2s, a2r, rts, rtr,
+    wgu, wd, mine, gext, ext_now, stage, rowact, rowcot, scl, part, own, r1, r2, ag, hs, rets, retr, dense, sibr, sall,
+    dgt, igt,
+    wsem, stsem, xsend, xrecv, gsend, grecv, bsend, brecv, r1s, r1r, r2s, r2r, a1s, a1r, a2s, a2r, rts, rtr,
     css, csr, osem,
 ):
     e = lax.axis_index("expert")
@@ -126,12 +179,11 @@
     closing = jnp.where(lane == TOK - 1, final_dev, (following != seg).astype(jnp.int32))
     live = jnp.maximum(jnp.broadcast_to(valid[...], (TOP, TOK)), closing).astype(F32)
     weight = jnp.minimum(jnp.exp(jnp.broadcast_to(log_ratio[...], (TOP, TOK))), 2.0) * live
-    slot_scale = (combine[...].T * weight).astype(BF)
+    slot_scale = (combine[...] * weight).astype(BF)
     count = jnp.broadcast_to(jnp.sum(live, axis=1, keepdims=True), (TOP, TOK)).astype(BF)
-    tail = pl.ds(2 * TOK, 2 * TOP)
-    mine[tail, :] = jnp.zeros((2 * TOP, width), BF)
-    mine[tail, pl.ds(0, TOK)] = jnp.concatenate([ids[...].astype(F32).T.astype(BF), slot_scale], axis=0)
-    mine[tail, pl.ds(TOK, TOK)] = jnp.concatenate([count, count], axis=0)
+    ids_scales = jnp.concatenate([ids[...].astype(F32).astype(BF), slot_scale], axis=0)
+    gext[c, 0, :, pl.ds(0, TOK)] = ids_scales
+    gext[c, 0, :, pl.ds(TOK, TOK)] = jnp.concatenate([count, count], axis=0)
     for cp in loads:
         cp.wait()
     pl.semaphore_wait(bar, len(partners))
@@ -196,10 +248,27 @@
             else:
                 send_half(*at, *rest)
 
+    def ext_copy(dz, dy):
+        n = dz * SIDE + dy
+        to = (-dz % SIDE) * SIDE + -dy % SIDE
+        return pltpu.make_async_remote_copy(
+            src_ref=gext.at[c, 0], dst_ref=gext.at[c, to], send_sem=xsend.at[n], recv_sem=xrecv.at[to],
+            device_id=sibling if n == 0 else peer(dz, dy), device_id_type=MESH,
+        )
+
+    def ext_relay():
+        others = gext.at[c, pl.ds(1, CHIPS - 1)]
+        return pltpu.make_async_remote_copy(
+            src_ref=others, dst_ref=others, send_sem=xsend.at[CHIPS], recv_sem=xrecv.at[CHIPS],
+            device_id=sibling, device_id_type=MESH,
+        )
+
+    offsets = [(dz, dy) for dz in range(SIDE) for dy in range(SIDE)]
+    ext_copy(0, 0).start()
     send_sibling(0, 0)
+    for at in offsets[1:]:
+        ext_copy(*at).start()
     send_full(0, 0, 0)
-
-    cnt[...] = jnp.zeros_like(cnt)
 
     row_i = lax.broadcasted_iota(jnp.int32, (TOK, TOK), 0)
     col_i = lax.broadcasted_iota(jnp.int32, (TOK, TOK), 1)
@@ -260,6 +329,9 @@
         copies = []
         for i, at in enumerate(elements):
             da, db = at
+            if at != (0, 0):
+                ext_now[i, 0] = gext[0, da * SIDE + db, :, pl.ds(0, TOK)]
+                ext_now[i, 1] = gext[1, db * SIDE + da, :, pl.ds(0, TOK)]
             theirs = (da * c + db * (1 - c)) * SIDE + da * (1 - c) + db * c
             ref = gbuf.at[1 - c, theirs]
             pltpu.make_async_copy(ref, ref, brecv.at[theirs]).wait()
@@ -281,9 +353,7 @@
         for i in range(n):
             picks, scales = [], []
             for core in range(2):
-                ext = stage[i, core, pl.ds(2 * TOK, 16), pl.ds(0, 2 * TOK)].astype(F32)
-                cnt[...] += ext[:, TOK:]
-                pick, scale = routing(ext[:, :TOK], expert, core)
+                pick, scale = routing(ext_now[i, core].astype(F32), expert, core)
                 picks.append(pick)
                 scales.append(jnp.sum(pick * scale, axis=1, keepdims=True))
             pick = jnp.concatenate(picks, axis=1).astype(BF)
@@ -394,48 +464,68 @@
         on((t >= 1) & (t < LAST), f, t, 2)
         on(t == LAST, f, t, 1)
 
+    def after(s, op):
+        for k, name in PASS_ON:
+            if name != op or (k == 0) != isinstance(s, int):
+                continue
+            if k == 0:
+                act_on(PASS_ON[k, name])
+            else:
+                on(s == k, act_on, PASS_ON[k, name])
+
     load_stage(CHUNK[0])
+    own_ext = gext.at[1 - c, 0]
+    pltpu.make_async_copy(own_ext, own_ext, xrecv.at[0]).wait()
+    ext_now[0] = gext[:, 0, :, pl.ds(0, TOK)]
+    after(0, "L")
     for cp in wcopies:
         cp.wait()
     forward(0, 1)
+    after(0, "F")
+    for n in range(1, CHIPS):
+        ref = gext.at[c, n]
+        pltpu.make_async_copy(ref, ref, xrecv.at[n]).wait()
+    ext_relay().start()
+    pass_sums(0, 1)
+    after(0, "S")
+    pointwise(0, 1)
+    after(0, "P")
     for core in range(2):
-        ext = stage[0, core, pl.ds(2 * TOK, 16), pl.ds(0, TOK)].astype(F32)
+        ext = ext_now[0, core].astype(F32)
         for k, (dz, dy) in enumerate(ORDER):
             expert = (2 * chip_at(-dz % SIDE, -dy % SIDE) + c).astype(F32)
             pick, _ = routing(ext, expert, core)
             sall[pl.ds(k * ROWS, ROWS), pl.ds(core * TOK, TOK)] = pick.astype(BF)
-    pass_sums(0, 1)
-    pointwise(0, 1)
+    after(0, "sall")
+    ext_relay().wait_recv()
 
     def step(s, carry):
+        any_size(s - 2, pointwise)
+        after(s, "P")
         any_size(s - 1, pass_sums)
-        any_size(s - 2, pointwise)
+        after(s, "S")
+        on((s >= 4) & (s < LAST + 3), backward, s - 3, 2)
+        on((s == 3) | (s == LAST + 3), backward, s - 3, 1)
+        after(s, "B")
         for k in range(1, LAST + 1):
-
-            @pl.when(s == k)
-            def _():
-                act_on(BEFORE.get(k, []))
-                load_stage(CHUNK[k])
-
+            on(s == k, load_stage, CHUNK[k])
+        after(s, "L")
         on(s == 3, sends_done, 0, 1)
         on((s >= 4) & (s <= LAST), sends_done, s - 3, 2)
         any_size(s, forward)
-        for k in AFTER:
-
-            @pl.when(s == k)
-            def _():
-                act_on(AFTER[k])
-
-        on(s == 1, pass_shares, 0, 1)
+        after(s, "F")
+        on(s == 2, pass_shares, 0, 1)
         any_size(s - 2, pass_shares)
-        t = s - 3
-        on((t >= 1) & (t < LAST), backward, t, 2)
-        on((t == 0) | (t == LAST), backward, t, 1)
+        after(s, "H")
         return carry
 
     lax.fori_loop(1, LAST + 4, step, 0)
 
-    factor = float(2 * CHIPS * TOK) / cnt[0:1, 0:1]
+    live_total = jnp.zeros((2 * TOP, TOK), F32)
+    for core in range(2):
+        for n in range(CHIPS):
+            live_total += gext[core, n, :, pl.ds(TOK, TOK)].astype(F32)
+    factor = float(2 * CHIPS * TOK) / live_total[0:1, 0:1]
     outs = []
     for f in range(4):
         if f >= 2:
@@ -473,6 +563,9 @@
     for k in range(1, CHIPS):
         ret_copy(k).wait_send()
 
+    for at in offsets:
+        ext_copy(*at).wait_send()
+    ext_relay().wait_send()
     for t in (6, 7):
         sends_done(t, 2)
     sends_done(LAST, 1)
@@ -510,6 +603,8 @@
             pltpu.VMEM((width, 2048), BF),
             pltpu.VMEM((1024, width), BF),
             pltpu.VMEM((BLOCK, width), BF),
+            pltpu.VMEM((2, CHIPS, 2 * TOP, 2 * TOK), BF),
+            pltpu.VMEM((2, 2, 2 * TOP, TOK), BF),
             pltpu.VMEM((2, 2, BLOCK, width), BF),
             pltpu.VMEM((2 * ROWS, width), BF),
             pltpu.VMEM((CHIPS * ROWS, width), BF),
@@ -527,8 +622,7 @@
             pltpu.VMEM((CHIPS * ROWS, 2 * TOK), BF),
             pltpu.VMEM((2, 256, width), BF),
             pltpu.VMEM((TOK, width), BF),
-            pltpu.VMEM((16, TOK), F32),
-            dma((17,)), dma((4,)),
+            dma((17,)), dma((4,)), dma((CHIPS + 1,)), dma((CHIPS + 1,)),
             dma((26 * 2,)), dma((CHIPS, 2)), dma((CHIPS,)), dma((CHIPS,)),
             dma((LAST + 1, 2)), dma((LAST + 1, 2)), dma((LAST + 1, 2)), dma((LAST + 1, 2)),
             dma((LAST + 1, 2)), dma((LAST + 1, 2)), dma((LAST + 1, 2)), dma((LAST + 1, 2)),
@@ -539,7 +633,7 @@
         ),
         cost_estimate=pl.CostEstimate(flops=28_200_000_000, bytes_accessed=60_000_000, transcendentals=1_000_000),
     )(
-        activations, cotangent, expert_ids, combine, log_ratio[None], valid_mask[None], segment_ids[None],
+        activations, cotangent, expert_ids.T, combine.T, log_ratio[None], valid_mask[None], segment_ids[None],
         w_gate, w_up, w_down,
     )
     return in_grad, down_grad

time: 214 us -> 194 us (0.907)
  the two profiles are of different devices: /device:TPU:107 before, /device:TPU:57 now
where the time goes in v3:
time: 194 us
  Pallas kernels  187 us (96%)
  local copies, waits for them, and re-layouts  5.93 us (3%)
    pallas_call x1, Pallas kernels, local(): pl.pallas_call(kernel, out_shape=(jax.ShapeDtypeStruct((tok_rows, width),...  187 us
    unnamed x2, local copies, waits for them, and re-layouts  5.93 us

profile of v3, /device:TPU:57, one launch (start us, length us, event | category | flops | bytes accessed | tf_op | source)
XLA Modules:
  0.0 194.0 jit_solution(15254365274395278769)
XLA Ops:
  0.6 187.5 %shard_map.113 = (bf16[128,1792]{1,0:T(8,128)(2,1)}, bf16[1,1024,1792]{2,1,0:T(8,128)(2,1)}, bf16[2,16,256,1792]{3,2,1,0:T(8,128)(2,1)}) custom-call(bf16[128,1792]{1,0:T(8,128)(2,1)} %acts.1, bf16[128,1792]{1,0:T(8,128)(2,1)} %cots.1, s32[8,128]{1,0:T(8,128)} %bitcast.5, f32[8,128]{1,0:T(8,128)} %bitcast.6, f32[1,128]{1,0:T(1,128)} %bitcast.7, ...), custom_call_target="tpu_custom_call" | custom-call | flops 28199999488 | bytes 60000000 | tf_op jit(solution)/shard_map/pallas_call | solution.py:593
  188.1 1.8 copy.14
  189.9 4.1 %copy.15 = bf16[1,1024,1792]{2,1,0:T(8,128)(2,1)} copy(bf16[1,1024,1792]{2,1,0:T(8,128)(2,1)} %get-tuple-element.9) | data formatting | bytes 7340032

commit v4 on v3

--- a/solution.py
+++ b/solution.py
@@ -119,7 +119,7 @@
 def kernel(
     acts, cots, ids, combine, log_ratio, valid, segments, w_gate, w_up, w_down,
     in_grad, down_grad, gbuf,
-    wgu, wd, mine, gext, ext_now, stage, rowact, rowcot, scl, part, own, r1, r2, ag, hs, rets, retr, dense, sibr, sall,
+    wgu, wd, mine, gext, ext_now, stage, rowact, rowcot, scl, part, own, r1, r2, ag, hs, rets, retr, dense, sibr, late, slate, sall,
     dgt, igt,
     wsem, stsem, xsend, xrecv, gsend, grecv, bsend, brecv, r1s, r1r, r2s, r2r, a1s, a1r, a2s, a2r, rts, rtr,
     css, csr, osem,
@@ -496,6 +496,11 @@
             expert = (2 * chip_at(-dz % SIDE, -dy % SIDE) + c).astype(F32)
             pick, _ = routing(ext, expert, core)
             sall[pl.ds(k * ROWS, ROWS), pl.ds(core * TOK, TOK)] = pick.astype(BF)
+    dz, dy = ORDER[-1]
+    twin = (2 * chip_at(-dz % SIDE, -dy % SIDE) + 1 - c).astype(F32)
+    pick0, _ = routing(ext_now[0, 0].astype(F32), twin, 0)
+    pick1, _ = routing(ext_now[0, 1].astype(F32), twin, 1)
+    slate[...] = jnp.where(c == 0, pick0, pick1).astype(BF)
     after(0, "sall")
     ext_relay().wait_recv()
 
@@ -535,9 +540,13 @@
         cp.start()
         outs.append(cp)
 
-    for k in range(CHIPS):
+    def returned(k):
         pltpu.make_async_copy(retr.at[k], retr.at[k], rtr.at[k]).wait()
-    dense[...] = dot(sall[...], retr[...].reshape(CHIPS * ROWS, width), 0, 0)
+
+    for k in range(CHIPS - 1):
+        returned(k)
+    early = (CHIPS - 1) * ROWS
+    dense[...] = dot(sall[pl.ds(0, early), :], retr[pl.ds(0, CHIPS - 1)].reshape(early, width), 0, 0)
     swap = pltpu.make_async_remote_copy(
         src_ref=dense.at[pl.ds(pl.multiple_of((1 - c) * TOK, TOK), TOK)],
         dst_ref=sibr,
@@ -547,9 +556,22 @@
         device_id_type=MESH,
     )
     swap.start()
+    returned(CHIPS - 1)
+    relay = pltpu.make_async_remote_copy(
+        src_ref=retr.at[CHIPS - 1],
+        dst_ref=late,
+        send_sem=css.at[1],
+        recv_sem=csr.at[1],
+        device_id=sibling,
+        device_id_type=MESH,
+    )
+    relay.start()
+    own_lanes = pl.ds(pl.multiple_of(c * TOK, TOK), TOK)
+    total = dense[own_lanes, :] + dot(sall[pl.ds(early, ROWS), own_lanes], retr[CHIPS - 1], 0, 0)
     swap.wait()
-    kept = dense[pl.ds(pl.multiple_of(c * TOK, TOK), TOK), :]
-    igt[...] = ((kept + sibr[...]) * factor).astype(BF)
+    relay.wait()
+    total = total + sibr[...] + dot(slate[...], late[...], 0, 0)
+    igt[...] = (total * factor).astype(BF)
     final = pltpu.make_async_copy(igt, in_grad, osem.at[2])
     final.start()
 
@@ -619,6 +641,8 @@
             pltpu.VMEM((CHIPS, ROWS, width), BF),
             pltpu.VMEM((2 * TOK, width), F32),
             pltpu.VMEM((TOK, width), F32),
+            pltpu.VMEM((ROWS, width), BF),
+            pltpu.VMEM((ROWS, TOK), BF),
             pltpu.VMEM((CHIPS * ROWS, 2 * TOK), BF),
             pltpu.VMEM((2, 256, width), BF),
             pltpu.VMEM((TOK, width), BF),
@@ -626,7 +650,7 @@
             dma((26 * 2,)), dma((CHIPS, 2)), dma((CHIPS,)), dma((CHIPS,)),
             dma((LAST + 1, 2)), dma((LAST + 1, 2)), dma((LAST + 1, 2)), dma((LAST + 1, 2)),
             dma((LAST + 1, 2)), dma((LAST + 1, 2)), dma((LAST + 1, 2)), dma((LAST + 1, 2)),
-            dma((CHIPS,)), dma((CHIPS,)), dma((1,)), dma((1,)), dma((3,)),
+            dma((CHIPS,)), dma((CHIPS,)), dma((2,)), dma((2,)), dma((3,)),
         ],
         compiler_params=pltpu.CompilerParams(
             collective_id=0, has_side_effects=True, vmem_limit_bytes=63 * 2**20

time: 194 us -> 192 us (0.990)
  Pallas kernels: 187 us -> 185 us
    pallas_call x1, Pallas kernels: 187 us -> 185 us  [local(): pl.pallas_call(kernel, out_shape=(jax.ShapeDtypeStruct((tok_rows, width),...]
where the time goes in v4:
time: 192 us
  Pallas kernels  185 us (96%)
  local copies, waits for them, and re-layouts  5.93 us (3%)
    pallas_call x1, Pallas kernels, local(): pl.pallas_call(kernel, out_shape=(jax.ShapeDtypeStruct((tok_rows, width),...  185 us
    unnamed x2, local copies, waits for them, and re-layouts  5.93 us

profile of v4, /device:TPU:57, one launch (start us, length us, event | category | flops | bytes accessed | tf_op | source)
XLA Modules:
  0.0 191.9 jit_solution(13689145266011068005)
XLA Ops:
  0.6 185.4 %shard_map.113 = (bf16[128,1792]{1,0:T(8,128)(2,1)}, bf16[1,1024,1792]{2,1,0:T(8,128)(2,1)}, bf16[2,16,256,1792]{3,2,1,0:T(8,128)(2,1)}) custom-call(bf16[128,1792]{1,0:T(8,128)(2,1)} %acts.1, bf16[128,1792]{1,0:T(8,128)(2,1)} %cots.1, s32[8,128]{1,0:T(8,128)} %bitcast.5, f32[8,128]{1,0:T(8,128)} %bitcast.6, f32[1,128]{1,0:T(1,128)} %bitcast.7, ...), custom_call_target="tpu_custom_call" | custom-call | flops 28199999488 | bytes 60000000 | tf_op jit(solution)/shard_map/pallas_call | solution.py:615
  186.0 1.8 copy.14
  187.8 4.1 %copy.15 = bf16[1,1024,1792]{2,1,0:T(8,128)(2,1)} copy(bf16[1,1024,1792]{2,1,0:T(8,128)(2,1)} %get-tuple-element.9) | data formatting | bytes 7340032

commit v5 on v4

--- a/solution.py
+++ b/solution.py
@@ -169,7 +169,7 @@
         pltpu.make_async_copy(acts, mine.at[pl.ds(0, TOK)], stsem.at[0]),
         pltpu.make_async_copy(cots, mine.at[pl.ds(TOK, TOK)], stsem.at[1]),
     ]
-    for cp in loads + wcopies:
+    for cp in loads:
         cp.start()
 
     lane = lax.broadcasted_iota(jnp.int32, (TOP, TOK), 1)
@@ -264,11 +264,13 @@
         )
 
     offsets = [(dz, dy) for dz in range(SIDE) for dy in range(SIDE)]
+    send_full(0, 0, 0)
     ext_copy(0, 0).start()
     send_sibling(0, 0)
+    for cp in wcopies:
+        cp.start()
     for at in offsets[1:]:
         ext_copy(*at).start()
-    send_full(0, 0, 0)
 
     row_i = lax.broadcasted_iota(jnp.int32, (TOK, TOK), 0)
     col_i = lax.broadcasted_iota(jnp.int32, (TOK, TOK), 1)

time: 192 us -> 197 us (1.026)
  Pallas kernels: 185 us -> 190 us
    pallas_call x1, Pallas kernels: 185 us -> 190 us  [local(): pl.pallas_call(kernel, out_shape=(jax.ShapeDtypeStruct((tok_rows, width),...]
where the time goes in v5:
time: 197 us
  Pallas kernels  190 us (96%)
  local copies, waits for them, and re-layouts  5.93 us (3%)
    pallas_call x1, Pallas kernels, local(): pl.pallas_call(kernel, out_shape=(jax.ShapeDtypeStruct((tok_rows, width),...  190 us
    unnamed x2, local copies, waits for them, and re-layouts  5.93 us

profile of v5, /device:TPU:57, one launch (start us, length us, event | category | flops | bytes accessed | tf_op | source)
XLA Modules:
  0.0 196.5 jit_solution(12089637086299245563)
XLA Ops:
  0.6 190.0 %shard_map.113 = (bf16[128,1792]{1,0:T(8,128)(2,1)}, bf16[1,1024,1792]{2,1,0:T(8,128)(2,1)}, bf16[2,16,256,1792]{3,2,1,0:T(8,128)(2,1)}) custom-call(bf16[128,1792]{1,0:T(8,128)(2,1)} %acts.1, bf16[128,1792]{1,0:T(8,128)(2,1)} %cots.1, s32[8,128]{1,0:T(8,128)} %bitcast.5, f32[8,128]{1,0:T(8,128)} %bitcast.6, f32[1,128]{1,0:T(1,128)} %bitcast.7, ...), custom_call_target="tpu_custom_call" | custom-call | flops 28199999488 | bytes 60000000 | tf_op jit(solution)/shard_map/pallas_call | solution.py:617
  190.6 1.8 copy.14
  192.4 4.1 %copy.15 = bf16[1,1024,1792]{2,1,0:T(8,128)(2,1)} copy(bf16[1,1024,1792]{2,1,0:T(8,128)(2,1)} %get-tuple-element.9) | data formatting | bytes 7340032
